TPU v7x, 128 devices: a whole 4x4x4 slice. The times are simulated.
128 devices in a mesh: gx: 8 (over z, core), gy: 16 (over y, x).
Axes of the slice: x: 4, y: 4, z: 4, core: 2. Of those that a mesh axis runs over, the one named last changes fastest.
Arguments:
- features: bfloat16 [131072, 512], P(('gx', 'gy')), may hold values from -6 to 6
- coefficients: bfloat16 [2048, 64, 512], P(('gx', 'gy')), may hold values from -0.25 to 0.25
- source_blocks: int32 [2048, 8], P(('gx', 'gy')), may hold values from 0 to 21, as said below
- send_x: int32 [128, 2, 1], P(('gx', 'gy')), may hold values from 0 to 15
- send_y: int32 [128, 2, 2], P(('gx', 'gy')), may hold values from 0 to 15
- node_counts: int32 [128], P(('gx', 'gy')), may hold values from 256 to 1024, as said below
- w_msg_in: bfloat16 [2, 512, 512], replicated, may hold values from -0.25 to 0.25
- w_msg_out: bfloat16 [2, 512, 512], replicated, may hold values from -0.25 to 0.25
- w_node_in: bfloat16 [2, 1024, 512], replicated, may hold values from -0.1875 to 0.1875
- b_node: float32 [2, 512], replicated, may hold values from -3 to 3
- w_node_out: bfloat16 [2, 512, 512], replicated, may hold values from -0.25 to 0.25
- ln_gain: float32 [2, 512], replicated, may hold values from 0.1 to 1.9
Outputs:
- latents: bfloat16 [131072, 512], P(('gx', 'gy'))
Inputs may be any that keep to these rules, and one draw needn't show every extreme that they name: `node_counts`: A partition's live nodes are its first slots; some partition is full and some holds a quarter of 1024. `source_blocks`: indices below 16 name local blocks, then 1 block from the lower and 1 from the upper first-direction neighbour, then 2 and 2 of the second direction; slots 0 to 5 of every block name local blocks, the last two slots name blocks received from neighbours. `send_x`: local block indices, repeats allowed. `send_y`: local block indices, repeats allowed.
All inputs are finite; a program needn't handle non-finite values.
Results may differ from a plain program's by a relative error of at most 0.013.
Values may be sent and summed in bfloat16 or wider, within the bound.
A program may use at most 64 MiB of HBM per device.

v0:
```python
import functools

import jax
import jax.numpy as jnp
from jax import lax
from jax.experimental import pallas as pl
from jax.experimental.pallas import tpu as pltpu
from jax.sharding import PartitionSpec as P

MESH = pl.DeviceIdType.MESH
F32 = jnp.float32
BF16 = jnp.bfloat16
FAR = 2


def dot(left, right):
    return jnp.dot(left, right, preferred_element_type=F32)


def silu(value):
    return value * jax.nn.sigmoid(value)


def normalised(raw):
    centred = raw - jnp.mean(raw, axis=1, keepdims=True)
    variance = jnp.mean(centred * centred, axis=1, keepdims=True)
    return centred * lax.rsqrt(variance + 1e-05)


def exchange_kernel(
    sources_in, send_x_in, send_y_in, counts, b_node_in, ln_gain_in,
    features, coefficients, w_msg_in, w_msg_out, w_node_in, w_node_out,
    last_hidden, last_states, last_w, last_row,
    sources, send_x, send_y, b_node, ln_gain,
    feat, coef, w_mi, w_mo, w_ni, w_no, merged, states, own, first_states, sent, halo_first, halo_second, base,
    small_sem, load_sem, send_sem, recv_sem,
):
    blocks, size, width = feat.shape
    n_sent = sent.shape[1]
    n_y = send_y.shape[1] * send_y.shape[2]
    near = sources.shape[0] - FAR
    halo = (halo_first, halo_second)
    i, j = lax.axis_index("gx"), lax.axis_index("gy")
    n_i, n_j = lax.axis_size("gx"), lax.axis_size("gy")

    smalls = [
        pltpu.make_async_copy(source, target, small_sem.at[n])
        for n, (source, target) in enumerate(
            [
                (sources_in, sources), (send_x_in, send_x), (send_y_in, send_y),
                (b_node_in, b_node), (ln_gain_in, ln_gain),
            ]
        )
    ]
    pairs = {
        "feat": (features, feat),
        "mi0": (w_msg_in.at[0], w_mi.at[0]),
        "mo0": (w_msg_out.at[0], w_mo.at[0]),
        "ni0": (w_node_in.at[0], w_ni.at[0]),
        "coef": (coefficients, coef),
        "no0": (w_node_out.at[0], w_no.at[0]),
        "mi1": (w_msg_in.at[1], w_mi.at[1]),
        "mo1": (w_msg_out.at[1], w_mo.at[1]),
        "ni1": (w_node_in.at[1], w_ni.at[1]),
        "no1": (w_node_out.at[1], last_w),
    }
    loads = {
        name: pltpu.make_async_copy(source, target, load_sem.at[n]) for n, (name, (source, target)) in enumerate(pairs.items())
    }
    loads["feat"].start()
    for copy in smalls:
        copy.start()
    for name in ("mi0", "mo0", "ni0"):
        loads[name].start()

    lower_x, upper_x = i > 0, i < n_i - 1
    lower_y, upper_y = j > 0, j < n_j - 1
    routes = [
        ((i, jnp.minimum(j + 1, n_j - 1)), upper_y, lower_y, 0, 2),
        ((i, jnp.maximum(j - 1, 0)), lower_y, upper_y, 2, 4),
        ((jnp.minimum(i + 1, n_i - 1), j), upper_x, lower_x, 4, 5),
        ((jnp.maximum(i - 1, 0), j), lower_x, upper_x, 5, 6),
    ]
    barrier = pltpu.get_barrier_semaphore()
    for device, there, _, _, _ in routes:

        @pl.when(there)
        def _():
            pl.semaphore_signal(barrier, inc=1, device_id=device, device_id_type=MESH)

    for _, _, comes, lo, hi in routes:

        @pl.when(jnp.logical_not(comes))
        def _():
            for buffer in halo:
                buffer[lo:hi] = jnp.zeros((hi - lo, size, width), BF16)

    def transfer(layer, n):
        device, there, comes, lo, hi = routes[n]
        copy = pltpu.make_async_remote_copy(
            src_ref=sent.at[layer, lo:hi],
            dst_ref=halo[layer].at[lo:hi],
            send_sem=send_sem.at[layer, n],
            recv_sem=recv_sem.at[layer, n],
            device_id=device,
            device_id_type=MESH,
        )
        return copy, there, comes

    def start(layer, routes_now):
        for n in routes_now:
            copy, there, _ = transfer(layer, n)
            pl.when(there)(copy.start)

    def receive(layer):
        for n in range(len(routes)):
            copy, _, comes = transfer(layer, n)
            pl.when(comes)(copy.wait_recv)

    def drain(layer):
        for n in range(len(routes)):
            copy, there, _ = transfer(layer, n)
            pl.when(there)(copy.wait_send)

    for copy in smalls:
        copy.wait()
    listed = [send_y[0, side, n] for side in (0, 1) for n in range(2)] + [send_x[0, 0, 0], send_x[0, 0, 1]]
    count = counts[0, 0]
    row = lax.broadcasted_iota(jnp.int32, (size, 1), 0)
    zero = jnp.zeros((), BF16)

    def live(block):
        return row + block * size < count

    def stacked(parts):
        return jnp.concatenate(parts, 0)

    def split(rows):
        return rows.reshape(rows.shape[0] // size, size, width)

    def outgoing(layer, rows):
        return dot(silu(dot(rows, w_mi[layer])).astype(BF16), merged[layer]).astype(BF16)

    def merge(layer):
        merged[layer] = dot(w_mo[layer], w_ni[layer, width:]).astype(BF16)

    def own_base(layer, rows_of):
        for lo in range(0, blocks, 4):
            rows = rows_of(lo, lo + 4)
            base[lo : lo + 4] = split(dot(rows, w_ni[layer, :width]) + b_node[layer][None, :])
        for block in range(blocks):
            picked = stacked([own[layer, sources[slot, block]] for slot in range(near)])
            base[block] += dot(coef[block, :, : near * size], picked)

    def pool_index(slot, block):
        index = sources[slot, block] - blocks
        return jnp.clip(jnp.where(index < 2, index + n_y, index - 2), 0, n_sent - 1)

    def activated(layer, block):
        picked = stacked([halo[layer][pool_index(slot, block)] for slot in range(near, near + FAR)])
        return silu(base[block] + dot(coef[block, :, near * size :], picked)).astype(BF16)

    def advanced(blocks_now, old):
        raw = dot(stacked([activated(0, block) for block in blocks_now]), w_no[0])
        alive = stacked([live(block) for block in blocks_now])
        return jnp.where(alive, old.astype(F32) + ln_gain[0][None, :] * normalised(raw), 0.0).astype(BF16)

    loads["feat"].wait()
    for n in range(n_sent):
        first_states[n] = jnp.where(live(listed[n]), feat[listed[n]], zero)
    for name in ("coef", "no0", "mi1", "mo1", "ni1", "no1"):
        loads[name].start()
    for name in ("mi0", "mo0", "ni0"):
        loads[name].wait()
    merge(0)
    sent[0] = split(outgoing(0, first_states[...].reshape(n_sent * size, width)))
    pl.semaphore_wait(barrier, sum(there.astype(jnp.int32) for _, there, _, _, _ in routes))
    start(0, (0, 1, 2, 3))

    for block in range(blocks):
        states[0, block] = jnp.where(live(block), feat[block], zero)
    for lo in range(0, blocks, 4):
        own[0, lo : lo + 4] = split(outgoing(0, states[0, lo : lo + 4].reshape(4 * size, width)))
    loads["coef"].wait()
    own_base(0, lambda lo, hi: states[0, lo:hi].reshape((hi - lo) * size, width))
    for name in ("no0", "mi1", "mo1", "ni1", "no1"):
        loads[name].wait()
    merge(1)

    receive(0)
    for lo, hi, routes_now in ((0, n_y, (0, 1)), (n_y, n_sent, (2, 3))):
        old = first_states[lo:hi].reshape((hi - lo) * size, width)
        sent[1, lo:hi] = split(outgoing(1, advanced(listed[lo:hi], old)))
        start(1, routes_now)

    for lo in range(0, blocks, 4):
        rows = slice(lo * size, (lo + 4) * size)
        last_states[rows] = advanced(range(lo, lo + 4), states[0, lo : lo + 4].reshape(4 * size, width))
    for lo in range(0, blocks, 4):
        own[1, lo : lo + 4] = split(outgoing(1, last_states[lo * size : (lo + 4) * size]))
    own_base(1, lambda lo, hi: last_states[lo * size : hi * size])
    last_row[0:1] = ln_gain[1:2]
    last_row[1:2] = jnp.full((1, width), count, jnp.int32).astype(F32)

    receive(1)
    for block in range(blocks):
        last_hidden[block * size : (block + 1) * size] = activated(1, block)
    drain(0)
    drain(1)


def last_kernel(last_hidden, last_states, last_w, last_row, out, latents, out_sem):
    nodes = last_states.shape[0]
    parts = out_sem.shape[0]
    step = nodes // parts
    gain, count = last_row[0:1], last_row[1:2]
    stores = []
    for n in range(parts):
        rows = slice(n * step, (n + 1) * step)
        normed = normalised(dot(last_hidden[rows], last_w[...]))
        position = lax.broadcasted_iota(jnp.int32, (step, 1), 0) + n * step
        alive = position.astype(F32) < count
        latents[rows] = jnp.where(alive, last_states[rows].astype(F32) + gain * normed, 0.0).astype(BF16)
        store = pltpu.make_async_copy(latents.at[rows], out.at[rows], out_sem.at[n])
        store.start()
        stores.append(store)
    for store in stores:
        store.wait()


def body(
    features, coefficients, source_blocks, send_x, send_y, node_counts,
    w_msg_in, w_msg_out, w_node_in, b_node, w_node_out, ln_gain,
):
    blocks, size, fan = coefficients.shape
    nodes, width = features.shape
    layers = w_msg_in.shape[0]
    n_sent = send_x.shape[1] * send_x.shape[2] + send_y.shape[1] * send_y.shape[2]
    any_, vmem = pl.BlockSpec(memory_space=pl.ANY), pl.BlockSpec(memory_space=pltpu.VMEM)
    operands = [
        source_blocks.T, send_x.transpose(0, 2, 1), send_y, node_counts.reshape(1, 1), b_node, ln_gain,
        features.reshape(blocks, size, width), coefficients, w_msg_in, w_msg_out, w_node_in, w_node_out,
    ]
    operands = [
        operand if operand.size == 1 else pltpu.with_memory_space_constraint(operand, pltpu.HBM) for operand in operands
    ]
    ints = [pltpu.SMEM(operand.shape, jnp.int32) for operand in operands[:3]]
    counted = pl.BlockSpec(memory_space=pltpu.SMEM)
    handed = [((nodes, width), BF16), ((nodes, width), BF16), ((width, width), BF16), ((8, width), F32)]
    between = pl.pallas_call(
        exchange_kernel,
        out_shape=[pltpu.VMEM(shape, dtype) for shape, dtype in handed],
        in_specs=[any_] * 3 + [counted] + [any_] * 8,
        out_specs=[vmem] * len(handed),
        scratch_shapes=ints
        + [
            pltpu.VMEM(b_node.shape, F32),
            pltpu.VMEM(ln_gain.shape, F32),
            pltpu.VMEM((blocks, size, width), BF16),
            pltpu.VMEM((blocks, size, fan), BF16),
            pltpu.VMEM(w_msg_in.shape, BF16),
            pltpu.VMEM(w_msg_out.shape, BF16),
            pltpu.VMEM(w_node_in.shape, BF16),
            pltpu.VMEM((1, width, width), BF16),
            pltpu.VMEM(w_msg_out.shape, BF16),
            pltpu.VMEM((1, blocks, size, width), BF16),
            pltpu.VMEM((layers, blocks, size, width), BF16),
            pltpu.VMEM((n_sent, size, width), BF16),
            pltpu.VMEM((layers, n_sent, size, width), BF16),
            pltpu.VMEM((n_sent, size, width), BF16),
            pltpu.VMEM((n_sent, size, width), BF16),
            pltpu.VMEM((blocks, size, width), F32),
            pltpu.SemaphoreType.DMA((5,)),
            pltpu.SemaphoreType.DMA((10,)),
            pltpu.SemaphoreType.DMA((layers, 4)),
            pltpu.SemaphoreType.DMA((layers, 4)),
        ],
        compiler_params=pltpu.CompilerParams(
            collective_id=0, has_side_effects=True, vmem_limit_bytes=40 * 2**20
        ),
        cost_estimate=pl.CostEstimate(flops=6 * 10**9, bytes_accessed=9 * 2**20, transcendentals=2 * 10**6),
        name="exchange",
    )(*operands)
    return pl.pallas_call(
        last_kernel,
        out_shape=jax.ShapeDtypeStruct((nodes, width), BF16),
        in_specs=[vmem] * len(handed),
        out_specs=any_,
        scratch_shapes=[pltpu.VMEM((nodes, width), BF16), pltpu.SemaphoreType.DMA((4,))],
        compiler_params=pltpu.CompilerParams(vmem_limit_bytes=40 * 2**20),
        cost_estimate=pl.CostEstimate(flops=6 * 10**8, bytes_accessed=2**20, transcendentals=10**3),
        name="last",
    )(*between)


def solution(mesh):
    split = ("gx", "gy")
    return jax.shard_map(
        body,
        mesh=mesh,
        in_specs=(
            P(split, None), P(split, None, None), P(split, None), P(split, None, None), P(split, None, None),
            P(split), P(), P(), P(), P(), P(), P(),
        ),
        out_specs=P(split, None),
        check_vma=False,
    )
```

profile of v0, /device:TPU:56, one launch (start us, length us, event | category | flops | bytes accessed | tf_op | source)
XLA Modules:
  0.0 19.3 jit_solution(16744839707403746025)
XLA Ops:
  0.7 16.7 %exchange.1 = (bf16[1024,512]{1,0:T(8,128)(2,1)S(1)}, bf16[1024,512]{1,0:T(8,128)(2,1)S(1)}, bf16[512,512]{1,0:T(8,128)(2,1)S(1)}, f32[8,512]{1,0:T(8,128)S(1)}) custom-call(s32[8,16]{1,0:T(8,128)} %bitcast.6, s32[1,1,2]{2,1,0:T(1,128)} %bitcast.7, s32[1,2,2]{2,1,0:T(2,128)} %send_y_in.1, s32[1,1]{1,0:T(1,128)} %bitcast.4.counts, f32[2,512]{1,0:T(2,128)} %b_node_in.1, ...), custom_call_target="tpu_custom_call" | custom-call | flops 6000000000 | bytes 9437184 | tf_op jit(solution)/shard_map/exchange/pallas_call | solution.py:250
  17.4 1.9 %last.1 = bf16[1024,512]{1,0:T(8,128)(2,1)} custom-call(bf16[1024,512]{1,0:T(8,128)(2,1)S(1)} %get-tuple-element.9.last_hidden, bf16[1024,512]{1,0:T(8,128)(2,1)S(1)} %get-tuple-element.10.last_states, bf16[512,512]{1,0:T(8,128)(2,1)S(1)} %get-tuple-element.11.last_w, f32[8,512]{1,0:T(8,128)S(1)} %get-tuple-element.12.last_row), custom_call_target="tpu_custom_call" | custom-call | flops 600000000 | bytes 1048576 | tf_op jit(solution)/shard_map/last/pallas_call | solution.py:284
where the time goes:
time: 19.4 us; the launch traced here: 19.3 us
  Pallas kernels  18.6 us (96%)
  between operations  0.66 us (3%)
    pallas_call x1, Pallas kernels, body(): pl.pallas_call(exchange_kernel, out_shape=[pltpu.VMEM(shape, dtype) for s...  16.7 us
    pallas_call x1, Pallas kernels, body(): pl.pallas_call(last_kernel, out_shape=jax.ShapeDtypeStruct((nodes, width)...  1.93 us

commit v1 on v0

--- a/solution.py
+++ b/solution.py
@@ -43,6 +43,21 @@
     i, j = lax.axis_index("gx"), lax.axis_index("gy")
     n_i, n_j = lax.axis_size("gx"), lax.axis_size("gy")
 
+    lower_x, upper_x = i > 0, i < n_i - 1
+    lower_y, upper_y = j > 0, j < n_j - 1
+    routes = [
+        ((i, jnp.minimum(j + 1, n_j - 1)), upper_y, lower_y, 0, 2),
+        ((i, jnp.maximum(j - 1, 0)), lower_y, upper_y, 2, 4),
+        ((jnp.minimum(i + 1, n_i - 1), j), upper_x, lower_x, 4, 5),
+        ((jnp.maximum(i - 1, 0), j), lower_x, upper_x, 5, 6),
+    ]
+    barrier = pltpu.get_barrier_semaphore()
+    for device, there, _, _, _ in routes:
+
+        @pl.when(there)
+        def _():
+            pl.semaphore_signal(barrier, inc=1, device_id=device, device_id_type=MESH)
+
     smalls = [
         pltpu.make_async_copy(source, target, small_sem.at[n])
         for n, (source, target) in enumerate(
@@ -53,10 +68,11 @@
         )
     ]
     pairs = {
+        "mo0": (w_msg_out.at[0], w_mo.at[0]),
+        "far0": (w_node_in.at[0, width:], w_ni.at[0, width:]),
         "feat": (features, feat),
         "mi0": (w_msg_in.at[0], w_mi.at[0]),
-        "mo0": (w_msg_out.at[0], w_mo.at[0]),
-        "ni0": (w_node_in.at[0], w_ni.at[0]),
+        "near0": (w_node_in.at[0, :width], w_ni.at[0, :width]),
         "coef": (coefficients, coef),
         "no0": (w_node_out.at[0], w_no.at[0]),
         "mi1": (w_msg_in.at[1], w_mi.at[1]),
@@ -67,26 +83,12 @@
     loads = {
         name: pltpu.make_async_copy(source, target, load_sem.at[n]) for n, (name, (source, target)) in enumerate(pairs.items())
     }
-    loads["feat"].start()
+    for name in ("mo0", "far0"):
+        loads[name].start()
     for copy in smalls:
         copy.start()
-    for name in ("mi0", "mo0", "ni0"):
+    for name in ("feat", "mi0"):
         loads[name].start()
-
-    lower_x, upper_x = i > 0, i < n_i - 1
-    lower_y, upper_y = j > 0, j < n_j - 1
-    routes = [
-        ((i, jnp.minimum(j + 1, n_j - 1)), upper_y, lower_y, 0, 2),
-        ((i, jnp.maximum(j - 1, 0)), lower_y, upper_y, 2, 4),
-        ((jnp.minimum(i + 1, n_i - 1), j), upper_x, lower_x, 4, 5),
-        ((jnp.maximum(i - 1, 0), j), lower_x, upper_x, 5, 6),
-    ]
-    barrier = pltpu.get_barrier_semaphore()
-    for device, there, _, _, _ in routes:
-
-        @pl.when(there)
-        def _():
-            pl.semaphore_signal(barrier, inc=1, device_id=device, device_id_type=MESH)
 
     for _, _, comes, lo, hi in routes:
 
@@ -122,6 +124,12 @@
             copy, there, _ = transfer(layer, n)
             pl.when(there)(copy.wait_send)
 
+    def merge(layer):
+        merged[layer] = dot(w_mo[layer], w_ni[layer, width:]).astype(BF16)
+
+    for name in ("mo0", "far0"):
+        loads[name].wait()
+    merge(0)
     for copy in smalls:
         copy.wait()
     listed = [send_y[0, side, n] for side in (0, 1) for n in range(2)] + [send_x[0, 0, 0], send_x[0, 0, 1]]
@@ -141,13 +149,10 @@
     def outgoing(layer, rows):
         return dot(silu(dot(rows, w_mi[layer])).astype(BF16), merged[layer]).astype(BF16)
 
-    def merge(layer):
-        merged[layer] = dot(w_mo[layer], w_ni[layer, width:]).astype(BF16)
-
-    def own_base(layer, rows_of):
-        for lo in range(0, blocks, 4):
-            rows = rows_of(lo, lo + 4)
-            base[lo : lo + 4] = split(dot(rows, w_ni[layer, :width]) + b_node[layer][None, :])
+    def rows_base(layer, rows):
+        return split(dot(rows, w_ni[layer, :width]) + b_node[layer][None, :])
+
+    def add_own(layer):
         for block in range(blocks):
             picked = stacked([own[layer, sources[slot, block]] for slot in range(near)])
             base[block] += dot(coef[block, :, : near * size], picked)
@@ -168,37 +173,67 @@
     loads["feat"].wait()
     for n in range(n_sent):
         first_states[n] = jnp.where(live(listed[n]), feat[listed[n]], zero)
-    for name in ("coef", "no0", "mi1", "mo1", "ni1", "no1"):
+    for name in ("near0", "coef", "no0", "mi1", "mo1", "ni1", "no1"):
         loads[name].start()
-    for name in ("mi0", "mo0", "ni0"):
-        loads[name].wait()
-    merge(0)
+    loads["mi0"].wait()
     sent[0] = split(outgoing(0, first_states[...].reshape(n_sent * size, width)))
     pl.semaphore_wait(barrier, sum(there.astype(jnp.int32) for _, there, _, _, _ in routes))
     start(0, (0, 1, 2, 3))
 
-    for block in range(blocks):
-        states[0, block] = jnp.where(live(block), feat[block], zero)
-    for lo in range(0, blocks, 4):
-        own[0, lo : lo + 4] = split(outgoing(0, states[0, lo : lo + 4].reshape(4 * size, width)))
-    loads["coef"].wait()
-    own_base(0, lambda lo, hi: states[0, lo:hi].reshape((hi - lo) * size, width))
+    def flat(values):
+        return values.reshape(values.shape[0] * size, width)
+
+    halves = [(0, 8), (8, 16)]
+
+    for lo, hi in halves:
+        for block in range(lo, hi):
+            states[0, block] = jnp.where(live(block), feat[block], zero)
+    raws = [dot(flat(states[0, lo:hi]), w_mi[0]) for lo, hi in halves]
+    for name in ("near0", "coef"):
+        loads[name].wait()
+    for (lo, hi), raw in zip(halves, raws):
+        base[lo:hi] = rows_base(0, flat(states[0, lo:hi]))
+        own[0, lo:hi] = split(dot(silu(raw).astype(BF16), merged[0]).astype(BF16))
     for name in ("no0", "mi1", "mo1", "ni1", "no1"):
         loads[name].wait()
     merge(1)
+    add_own(0)
 
     receive(0)
-    for lo, hi, routes_now in ((0, n_y, (0, 1)), (n_y, n_sent, (2, 3))):
-        old = first_states[lo:hi].reshape((hi - lo) * size, width)
-        sent[1, lo:hi] = split(outgoing(1, advanced(listed[lo:hi], old)))
-        start(1, routes_now)
-
-    for lo in range(0, blocks, 4):
-        rows = slice(lo * size, (lo + 4) * size)
-        last_states[rows] = advanced(range(lo, lo + 4), states[0, lo : lo + 4].reshape(4 * size, width))
-    for lo in range(0, blocks, 4):
-        own[1, lo : lo + 4] = split(outgoing(1, last_states[lo * size : (lo + 4) * size]))
-    own_base(1, lambda lo, hi: last_states[lo * size : hi * size])
+
+    def next_states(groups, olds):
+        hiddens = [stacked([activated(0, block) for block in group]) for group in groups]
+        raws = [dot(value, w_no[0]) for value in hiddens]
+        news = []
+        for group, old, raw in zip(groups, olds, raws):
+            alive = stacked([live(block) for block in group])
+            value = old().astype(F32) + ln_gain[0][None, :] * normalised(raw)
+            news.append(jnp.where(alive, value, 0.0).astype(BF16))
+        return news
+
+    groups = [(0, 1), (2, 3), (4, 5)]
+    news = next_states(
+        [[listed[n] for n in group] for group in groups],
+        [lambda group=group: stacked([first_states[n] for n in group]) for group in groups],
+    )
+    raws = [dot(new, w_mi[1]) for new in news]
+    for group, raw in zip(groups, raws):
+        rows = split(dot(silu(raw).astype(BF16), merged[1]).astype(BF16))
+        for n, row_block in zip(group, rows):
+            sent[1, n] = row_block
+    start(1, (0, 1, 2, 3))
+
+    news = next_states(
+        [range(lo, hi) for lo, hi in halves], [lambda lo=lo, hi=hi: flat(states[0, lo:hi]) for lo, hi in halves]
+    )
+    raws = []
+    for (lo, hi), new in zip(halves, news):
+        last_states[lo * size : hi * size] = new
+        raws.append(dot(new, w_mi[1]))
+    for (lo, hi), new, raw in zip(halves, news, raws):
+        base[lo:hi] = rows_base(1, new)
+        own[1, lo:hi] = split(dot(silu(raw).astype(BF16), merged[1]).astype(BF16))
+    add_own(1)
     last_row[0:1] = ln_gain[1:2]
     last_row[1:2] = jnp.full((1, width), count, jnp.int32).astype(F32)
 
@@ -271,7 +306,7 @@
             pltpu.VMEM((n_sent, size, width), BF16),
             pltpu.VMEM((blocks, size, width), F32),
             pltpu.SemaphoreType.DMA((5,)),
-            pltpu.SemaphoreType.DMA((10,)),
+            pltpu.SemaphoreType.DMA((11,)),
             pltpu.SemaphoreType.DMA((layers, 4)),
             pltpu.SemaphoreType.DMA((layers, 4)),
         ],

time: 19.4 us -> 18.2 us (0.938)
  Pallas kernels: 18.6 us -> 17.4 us
    pallas_call x1, Pallas kernels: 16.7 us -> 15.4 us  [body(): pl.pallas_call(exchange_kernel, out_shape=[pltpu.VMEM(shape, dtype) for s...]
where the time goes in v1:
time: 18.2 us; the launch traced here: 18 us
  Pallas kernels  17.4 us (96%)
  between operations  0.66 us (4%)
    pallas_call x1, Pallas kernels, body(): pl.pallas_call(exchange_kernel, out_shape=[pltpu.VMEM(shape, dtype) for s...  15.4 us
    pallas_call x1, Pallas kernels, body(): pl.pallas_call(last_kernel, out_shape=jax.ShapeDtypeStruct((nodes, width)...  1.93 us

profile of v1, /device:TPU:56, one launch (start us, length us, event | category | flops | bytes accessed | tf_op | source)
XLA Modules:
  0.0 18.0 jit_solution(17316687288246381616)
XLA Ops:
  0.7 15.4 %exchange.1 = (bf16[1024,512]{1,0:T(8,128)(2,1)S(1)}, bf16[1024,512]{1,0:T(8,128)(2,1)S(1)}, bf16[512,512]{1,0:T(8,128)(2,1)S(1)}, f32[8,512]{1,0:T(8,128)S(1)}) custom-call(s32[8,16]{1,0:T(8,128)} %bitcast.6, s32[1,1,2]{2,1,0:T(1,128)} %bitcast.7, s32[1,2,2]{2,1,0:T(2,128)} %send_y_in.1, s32[1,1]{1,0:T(1,128)} %bitcast.4.counts, f32[2,512]{1,0:T(2,128)} %b_node_in.1, ...), custom_call_target="tpu_custom_call" | custom-call | flops 6000000000 | bytes 9437184 | tf_op jit(solution)/shard_map/exchange/pallas_call | solution.py:285
  16.1 1.9 %last.1 = bf16[1024,512]{1,0:T(8,128)(2,1)} custom-call(bf16[1024,512]{1,0:T(8,128)(2,1)S(1)} %get-tuple-element.9.last_hidden, bf16[1024,512]{1,0:T(8,128)(2,1)S(1)} %get-tuple-element.10.last_states, bf16[512,512]{1,0:T(8,128)(2,1)S(1)} %get-tuple-element.11.last_w, f32[8,512]{1,0:T(8,128)S(1)} %get-tuple-element.12.last_row), custom_call_target="tpu_custom_call" | custom-call | flops 600000000 | bytes 1048576 | tf_op jit(solution)/shard_map/last/pallas_call | solution.py:319

commit v2 on v1

--- a/solution.py
+++ b/solution.py
@@ -21,10 +21,13 @@
     return value * jax.nn.sigmoid(value)
 
 
+def centred(weight):
+    weight = weight.astype(F32)
+    return (weight - jnp.mean(weight, axis=1, keepdims=True)).astype(BF16)
+
+
 def normalised(raw):
-    centred = raw - jnp.mean(raw, axis=1, keepdims=True)
-    variance = jnp.mean(centred * centred, axis=1, keepdims=True)
-    return centred * lax.rsqrt(variance + 1e-05)
+    return raw * lax.rsqrt(jnp.mean(raw * raw, axis=1, keepdims=True) + 1e-05)
 
 
 def exchange_kernel(
@@ -32,7 +35,7 @@
     features, coefficients, w_msg_in, w_msg_out, w_node_in, w_node_out,
     last_hidden, last_states, last_w, last_row,
     sources, send_x, send_y, b_node, ln_gain,
-    feat, coef, w_mi, w_mo, w_ni, w_no, merged, states, own, first_states, sent, halo_first, halo_second, base,
+    feat, coef, w_mi, w_mo, w_ni, w_no, first_w, merged, states, own, first_states, sent, halo_first, halo_second, base,
     small_sem, load_sem, send_sem, recv_sem,
 ):
     blocks, size, width = feat.shape
@@ -78,7 +81,7 @@
         "mi1": (w_msg_in.at[1], w_mi.at[1]),
         "mo1": (w_msg_out.at[1], w_mo.at[1]),
         "ni1": (w_node_in.at[1], w_ni.at[1]),
-        "no1": (w_node_out.at[1], last_w),
+        "no1": (w_node_out.at[1], w_no.at[1]),
     }
     loads = {
         name: pltpu.make_async_copy(source, target, load_sem.at[n]) for n, (name, (source, target)) in enumerate(pairs.items())
@@ -110,14 +113,32 @@
         return copy, there, comes
 
     def start(layer, routes_now):
-        for n in routes_now:
-            copy, there, _ = transfer(layer, n)
-            pl.when(there)(copy.start)
+        inner = functools.reduce(jnp.logical_and, [route[1] for route in routes])
+
+        @pl.when(inner)
+        def _():
+            for n in routes_now:
+                transfer(layer, n)[0].start()
+
+        @pl.when(jnp.logical_not(inner))
+        def _():
+            for n in routes_now:
+                copy, there, _ = transfer(layer, n)
+                pl.when(there)(copy.start)
 
     def receive(layer):
-        for n in range(len(routes)):
-            copy, _, comes = transfer(layer, n)
-            pl.when(comes)(copy.wait_recv)
+        inner = functools.reduce(jnp.logical_and, [route[1] for route in routes])
+
+        @pl.when(inner)
+        def _():
+            for n in range(len(routes)):
+                transfer(layer, n)[0].wait_recv()
+
+        @pl.when(jnp.logical_not(inner))
+        def _():
+            for n in range(len(routes)):
+                copy, _, comes = transfer(layer, n)
+                pl.when(comes)(copy.wait_recv)
 
     def drain(layer):
         for n in range(len(routes)):
@@ -197,13 +218,15 @@
     for name in ("no0", "mi1", "mo1", "ni1", "no1"):
         loads[name].wait()
     merge(1)
+    first_w[...] = centred(w_no[0])
+    last_w[...] = centred(w_no[1])
     add_own(0)
 
     receive(0)
 
     def next_states(groups, olds):
         hiddens = [stacked([activated(0, block) for block in group]) for group in groups]
-        raws = [dot(value, w_no[0]) for value in hiddens]
+        raws = [dot(value, first_w[...]) for value in hiddens]
         news = []
         for group, old, raw in zip(groups, olds, raws):
             alive = stacked([live(block) for block in group])
@@ -296,7 +319,8 @@
             pltpu.VMEM(w_msg_in.shape, BF16),
             pltpu.VMEM(w_msg_out.shape, BF16),
             pltpu.VMEM(w_node_in.shape, BF16),
-            pltpu.VMEM((1, width, width), BF16),
+            pltpu.VMEM(w_node_out.shape, BF16),
+            pltpu.VMEM((width, width), BF16),
             pltpu.VMEM(w_msg_out.shape, BF16),
             pltpu.VMEM((1, blocks, size, width), BF16),
             pltpu.VMEM((layers, blocks, size, width), BF16),

time: 18.2 us -> 17.8 us (0.978)
  Pallas kernels: 17.4 us -> 17 us
    pallas_call x1, Pallas kernels: 15.4 us -> 15.2 us  [body(): pl.pallas_call(exchange_kernel, out_shape=[pltpu.VMEM(shape, dtype) for s...]
where the time goes in v2:
time: 17.8 us; the launch traced here: 17.7 us
  Pallas kernels  17 us (96%)
  between operations  0.66 us (4%)
    pallas_call x1, Pallas kernels, body(): pl.pallas_call(exchange_kernel, out_shape=[pltpu.VMEM(shape, dtype) for s...  15.2 us
    pallas_call x1, Pallas kernels, body(): pl.pallas_call(last_kernel, out_shape=jax.ShapeDtypeStruct((nodes, width)...  1.81 us

profile of v2, /device:TPU:56, one launch (start us, length us, event | category | flops | bytes accessed | tf_op | source)
XLA Modules:
  0.0 17.7 jit_solution(3089622530264634789)
XLA Ops:
  0.7 15.2 %exchange.1 = (bf16[1024,512]{1,0:T(8,128)(2,1)S(1)}, bf16[1024,512]{1,0:T(8,128)(2,1)S(1)}, bf16[512,512]{1,0:T(8,128)(2,1)S(1)}, f32[8,512]{1,0:T(8,128)S(1)}) custom-call(s32[8,16]{1,0:T(8,128)} %bitcast.6, s32[1,1,2]{2,1,0:T(1,128)} %bitcast.7, s32[1,2,2]{2,1,0:T(2,128)} %send_y_in.1, s32[1,1]{1,0:T(1,128)} %bitcast.4.counts, f32[2,512]{1,0:T(2,128)} %b_node_in.1, ...), custom_call_target="tpu_custom_call" | custom-call | flops 6000000000 | bytes 9437184 | tf_op jit(solution)/shard_map/exchange/pallas_call | solution.py:308
  15.9 1.8 %last.1 = bf16[1024,512]{1,0:T(8,128)(2,1)} custom-call(bf16[1024,512]{1,0:T(8,128)(2,1)S(1)} %get-tuple-element.9.last_hidden, bf16[1024,512]{1,0:T(8,128)(2,1)S(1)} %get-tuple-element.10.last_states, bf16[512,512]{1,0:T(8,128)(2,1)S(1)} %get-tuple-element.11.last_w, f32[8,512]{1,0:T(8,128)S(1)} %get-tuple-element.12.last_row), custom_call_target="tpu_custom_call" | custom-call | flops 600000000 | bytes 1048576 | tf_op jit(solution)/shard_map/last/pallas_call | solution.py:343

commit v3 on v2

--- a/solution.py
+++ b/solution.py
@@ -33,9 +33,9 @@
 def exchange_kernel(
     sources_in, send_x_in, send_y_in, counts, b_node_in, ln_gain_in,
     features, coefficients, w_msg_in, w_msg_out, w_node_in, w_node_out,
-    last_hidden, last_states, last_w, last_row,
+    halo_second, base, coef, last_states, last_w, last_row, picks,
     sources, send_x, send_y, b_node, ln_gain,
-    feat, coef, w_mi, w_mo, w_ni, w_no, first_w, merged, states, own, first_states, sent, halo_first, halo_second, base,
+    feat, w_mi, w_mo, w_ni, w_no, first_w, merged, states, own, first_states, sent, halo_first,
     small_sem, load_sem, send_sem, recv_sem,
 ):
     blocks, size, width = feat.shape
@@ -260,25 +260,34 @@
     last_row[0:1] = ln_gain[1:2]
     last_row[1:2] = jnp.full((1, width), count, jnp.int32).astype(F32)
 
+    for block in range(blocks):
+        for slot in range(near, near + FAR):
+            picks[slot - near, block] = pool_index(slot, block)
     receive(1)
-    for block in range(blocks):
-        last_hidden[block * size : (block + 1) * size] = activated(1, block)
     drain(0)
     drain(1)
 
 
-def last_kernel(last_hidden, last_states, last_w, last_row, out, latents, out_sem):
-    nodes = last_states.shape[0]
+def last_kernel(halo, base, coef, last_states, last_w, last_row, picks, out, latents, out_sem):
+    blocks, size, width = base.shape
+    near = coef.shape[2] - FAR * size
+    gain, count = last_row[0:1], last_row[1:2]
     parts = out_sem.shape[0]
-    step = nodes // parts
-    gain, count = last_row[0:1], last_row[1:2]
+    step = blocks // parts
+
+    def activated(block):
+        picked = jnp.concatenate([halo[picks[slot, block]] for slot in range(FAR)], 0)
+        return silu(base[block] + dot(coef[block, :, near:], picked)).astype(BF16)
+
+    hiddens = [jnp.concatenate([activated(block) for block in range(n * step, (n + 1) * step)], 0) for n in range(parts)]
+    raws = [dot(value, last_w[...]) for value in hiddens]
     stores = []
-    for n in range(parts):
-        rows = slice(n * step, (n + 1) * step)
-        normed = normalised(dot(last_hidden[rows], last_w[...]))
-        position = lax.broadcasted_iota(jnp.int32, (step, 1), 0) + n * step
+    for n, raw in enumerate(raws):
+        rows = slice(n * step * size, (n + 1) * step * size)
+        position = lax.broadcasted_iota(jnp.int32, (step * size, 1), 0) + n * step * size
         alive = position.astype(F32) < count
-        latents[rows] = jnp.where(alive, last_states[rows].astype(F32) + gain * normed, 0.0).astype(BF16)
+        value = last_states[rows].astype(F32) + gain * normalised(raw)
+        latents[rows] = jnp.where(alive, value, 0.0).astype(BF16)
         store = pltpu.make_async_copy(latents.at[rows], out.at[rows], out_sem.at[n])
         store.start()
         stores.append(store)
@@ -290,7 +299,7 @@
     features, coefficients, source_blocks, send_x, send_y, node_counts,
     w_msg_in, w_msg_out, w_node_in, b_node, w_node_out, ln_gain,
 ):
-    blocks, size, fan = coefficients.shape
+    blocks, size, _ = coefficients.shape
     nodes, width = features.shape
     layers = w_msg_in.shape[0]
     n_sent = send_x.shape[1] * send_x.shape[2] + send_y.shape[1] * send_y.shape[2]
@@ -304,18 +313,26 @@
     ]
     ints = [pltpu.SMEM(operand.shape, jnp.int32) for operand in operands[:3]]
     counted = pl.BlockSpec(memory_space=pltpu.SMEM)
-    handed = [((nodes, width), BF16), ((nodes, width), BF16), ((width, width), BF16), ((8, width), F32)]
+    handed = [
+        pltpu.VMEM((n_sent, size, width), BF16),
+        pltpu.VMEM((blocks, size, width), F32),
+        pltpu.VMEM(coefficients.shape, BF16),
+        pltpu.VMEM((nodes, width), BF16),
+        pltpu.VMEM((width, width), BF16),
+        pltpu.VMEM((8, width), F32),
+        pltpu.SMEM((FAR, blocks), jnp.int32),
+    ]
+    spaces = [vmem] * 6 + [pl.BlockSpec(memory_space=pltpu.SMEM)]
     between = pl.pallas_call(
         exchange_kernel,
-        out_shape=[pltpu.VMEM(shape, dtype) for shape, dtype in handed],
+        out_shape=handed,
         in_specs=[any_] * 3 + [counted] + [any_] * 8,
-        out_specs=[vmem] * len(handed),
+        out_specs=spaces,
         scratch_shapes=ints
         + [
             pltpu.VMEM(b_node.shape, F32),
             pltpu.VMEM(ln_gain.shape, F32),
             pltpu.VMEM((blocks, size, width), BF16),
-            pltpu.VMEM((blocks, size, fan), BF16),
             pltpu.VMEM(w_msg_in.shape, BF16),
             pltpu.VMEM(w_msg_out.shape, BF16),
             pltpu.VMEM(w_node_in.shape, BF16),
@@ -327,8 +344,6 @@
             pltpu.VMEM((n_sent, size, width), BF16),
             pltpu.VMEM((layers, n_sent, size, width), BF16),
             pltpu.VMEM((n_sent, size, width), BF16),
-            pltpu.VMEM((n_sent, size, width), BF16),
-            pltpu.VMEM((blocks, size, width), F32),
             pltpu.SemaphoreType.DMA((5,)),
             pltpu.SemaphoreType.DMA((11,)),
             pltpu.SemaphoreType.DMA((layers, 4)),
@@ -343,7 +358,7 @@
     return pl.pallas_call(
         last_kernel,
         out_shape=jax.ShapeDtypeStruct((nodes, width), BF16),
-        in_specs=[vmem] * len(handed),
+        in_specs=spaces,
         out_specs=any_,
         scratch_shapes=[pltpu.VMEM((nodes, width), BF16), pltpu.SemaphoreType.DMA((4,))],
         compiler_params=pltpu.CompilerParams(vmem_limit_bytes=40 * 2**20),

time: 17.8 us -> 17.7 us (level)
    pallas_call x1, Pallas kernels: 15.2 us -> 14.7 us  [body(): pl.pallas_call(exchange_kernel, out_shape=handed, in_specs=[any_] * 3 + [...]
    pallas_call x1, Pallas kernels: 1.81 us -> 2.17 us  [body(): pl.pallas_call(last_kernel, out_shape=jax.ShapeDtypeStruct((nodes, width)...]
where the time goes in v3:
time: 17.7 us; the launch traced here: 17.6 us
  Pallas kernels  16.9 us (95%)
  between operations  0.66 us (4%)
    pallas_call x1, Pallas kernels, body(): pl.pallas_call(exchange_kernel, out_shape=handed, in_specs=[any_] * 3 + [...  14.7 us
    pallas_call x1, Pallas kernels, body(): pl.pallas_call(last_kernel, out_shape=jax.ShapeDtypeStruct((nodes, width)...  2.17 us

profile of v3, /device:TPU:56, one launch (start us, length us, event | category | flops | bytes accessed | tf_op | source)
XLA Modules:
  0.0 17.6 jit_solution(8912476773066461561)
XLA Ops:
  0.7 14.7 %exchange.1 = (bf16[6,64,512]{2,1,0:T(8,128)(2,1)S(1)}, f32[16,64,512]{2,1,0:T(8,128)S(1)}, bf16[16,64,512]{2,1,0:T(8,128)(2,1)S(1)}, bf16[1024,512]{1,0:T(8,128...) custom-call(s32[8,16]{1,0:T(8,128)} %bitcast.6, s32[1,1,2]{2,1,0:T(1,128)} %bitcast.7, ...), custom_call_target="tpu_custom_call" | custom-call | flops 6000000000 | bytes 9437184 | tf_op jit(solution)/shard_map/exchange/pallas_call | solution.py:326
  15.4 2.2 %last.1 = bf16[1024,512]{1,0:T(8,128)(2,1)} custom-call(bf16[6,64,512]{2,1,0:T(8,128)(2,1)S(1)} %get-tuple-element.12.halo, f32[16,64,512]{2,1,0:T(8,128)S(1)} %get-tuple-element.13.base, bf16[16,64,512]{2,1,0:T(8,128)(2,1)S(1)} %get-tuple-element.14.coef, bf16[1024,512]{1,0:T(8,128)(2,1)S(1)} %get-tuple-element.15.last_states, ...), custom_call_target="tpu_custom_call" | custom-call | flops 600000000 | bytes 1048576 | tf_op jit(solution)/shard_map/last/pallas_call | solution.py:358

commit v4 on v3

--- a/solution.py
+++ b/solution.py
@@ -204,7 +204,7 @@
     def flat(values):
         return values.reshape(values.shape[0] * size, width)
 
-    halves = [(0, 8), (8, 16)]
+    halves = [(0, 16)]
 
     for lo, hi in halves:
         for block in range(lo, hi):
@@ -257,6 +257,7 @@
         base[lo:hi] = rows_base(1, new)
         own[1, lo:hi] = split(dot(silu(raw).astype(BF16), merged[1]).astype(BF16))
     add_own(1)
+    drain(0)
     last_row[0:1] = ln_gain[1:2]
     last_row[1:2] = jnp.full((1, width), count, jnp.int32).astype(F32)
 
@@ -264,7 +265,6 @@
         for slot in range(near, near + FAR):
             picks[slot - near, block] = pool_index(slot, block)
     receive(1)
-    drain(0)
     drain(1)
 
 

time: 17.7 us -> 17.7 us (level)
  no operation moved by 1% of the time
where the time goes in v4:
time: 17.7 us; the launch traced here: 17.6 us
  Pallas kernels  16.9 us (95%)
  between operations  0.66 us (4%)
    pallas_call x1, Pallas kernels, body(): pl.pallas_call(exchange_kernel, out_shape=handed, in_specs=[any_] * 3 + [...  14.8 us
    pallas_call x1, Pallas kernels, body(): pl.pallas_call(last_kernel, out_shape=jax.ShapeDtypeStruct((nodes, width)...  2.14 us

profile of v4, /device:TPU:56, one launch (start us, length us, event | category | flops | bytes accessed | tf_op | source)
XLA Modules:
  0.0 17.6 jit_solution(2654672258523757123)
XLA Ops:
  0.7 14.8 %exchange.1 = (bf16[6,64,512]{2,1,0:T(8,128)(2,1)S(1)}, f32[16,64,512]{2,1,0:T(8,128)S(1)}, bf16[16,64,512]{2,1,0:T(8,128)(2,1)S(1)}, bf16[1024,512]{1,0:T(8,128...) custom-call(s32[8,16]{1,0:T(8,128)} %bitcast.6, s32[1,1,2]{2,1,0:T(1,128)} %bitcast.7, ...), custom_call_target="tpu_custom_call" | custom-call | flops 6000000000 | bytes 9437184 | tf_op jit(solution)/shard_map/exchange/pallas_call | solution.py:326
  15.4 2.1 %last.1 = bf16[1024,512]{1,0:T(8,128)(2,1)} custom-call(bf16[6,64,512]{2,1,0:T(8,128)(2,1)S(1)} %get-tuple-element.12.halo, f32[16,64,512]{2,1,0:T(8,128)S(1)} %get-tuple-element.13.base, bf16[16,64,512]{2,1,0:T(8,128)(2,1)S(1)} %get-tuple-element.14.coef, bf16[1024,512]{1,0:T(8,128)(2,1)S(1)} %get-tuple-element.15.last_states, ...), custom_call_target="tpu_custom_call" | custom-call | flops 600000000 | bytes 1048576 | tf_op jit(solution)/shard_map/last/pallas_call | solution.py:358
